TPU v7x, 32 devices: a whole 2x2x4 slice. The times are simulated.
32 devices in a mesh: row: 4 (over z), col: 8 (over y, x, core).
Axes of the slice: x: 2, y: 2, z: 4, core: 2. Of those that a mesh axis runs over, the one named last changes fastest.
Arguments:
- activations: bfloat16 [1024, 28672], P(('row', 'col')), may hold values from -6 to 6
- gradients: bfloat16 [1024, 8192], P(('row', 'col')), may hold values from -6 to 6
- act_basis: bfloat16 [28672, 28672], P('col', 'row'), may hold values from -0.03125 to 0.03125
- grad_basis: bfloat16 [8192, 8192], P('row', 'col'), may hold values from -0.0625 to 0.0625
Outputs:
- correction: float32 [28672, 8192], P('row', 'col')
All inputs are finite; a program needn't handle non-finite values.
Results may differ from a plain program's by a relative error of at most 0.0041.
Values may be sent and summed in bfloat16 or wider, within the bound.
A program may use at most 192 MiB of HBM per device.

v0:
```python
import jax
import jax.numpy as jnp
from jax import lax
from jax.sharding import PartitionSpec as P

SEQS = 2
LEN = 512


def on_device(activations, gradients, act_basis, grad_basis):
    local_acts = lax.all_to_all(activations, "col", split_axis=1, concat_axis=0, tiled=True)
    whole_acts = lax.all_gather(local_acts, "row", axis=0, tiled=True)
    shares = lax.psum_scatter(
        jnp.dot(whole_acts, act_basis, preferred_element_type=jnp.float32),
        "col",
        scatter_dimension=0,
        tiled=True,
    )
    rotated = lax.all_gather(shares.astype(jnp.bfloat16), "col", axis=0, tiled=True)
    grad_block = lax.all_gather(gradients, "col", axis=0, tiled=True)
    local_grads = lax.all_to_all(grad_block, "row", split_axis=1, concat_axis=0, tiled=True)
    partial_grads = jnp.dot(local_grads, grad_basis, preferred_element_type=jnp.float32)
    rot_grads = lax.psum(partial_grads, "row").astype(jnp.bfloat16)
    total = jnp.zeros((rotated.shape[1], rot_grads.shape[1]), jnp.float32)
    for seq in range(SEQS):
        left = rotated[seq * LEN : (seq + 1) * LEN]
        right = rot_grads[seq * LEN : (seq + 1) * LEN]
        grad_s = lax.dot_general(
            left, right, (((0,), (0,)), ((), ())), preferred_element_type=jnp.float32
        )
        total = total + grad_s * grad_s
    return total * (1.0 / (SEQS * LEN))


def solution(mesh):
    return jax.shard_map(
        on_device,
        mesh=mesh,
        in_specs=(
            P(("row", "col"), None),
            P(("row", "col"), None),
            P("col", "row"),
            P("row", "col"),
        ),
        out_specs=P("row", "col"),
        check_vma=False,
    )
```

profile of v0, /device:TPU:0, one launch (start us, length us, event | category | flops | bytes accessed | tf_op | source)
XLA Modules:
  0.0 761.4 jit_solution(148176985733283894)
XLA Ops:
  6.5 0.0 all-gather.4.cloned.1.call-start
  6.5 1.7 copy.13
  8.2 28.9 %all_to_all.38 = bf16[32,8,3584]{2,0,1:T(8,128)(2,1)} all-to-all(bf16[32,8,3584]{2,0,1:T(8,128)(2,1)S(1)} %bitcast.17), channel_id=1, replica_groups=mesh['row'=4,'col'=8] {'col'}, dimensions={1} | all-to-all | bytes 3670016 | tf_op jit(solution)/shard_map/all_to_all | solution.py:11
  37.1 0.0 all-gather.4.cloned.1.call-update
  37.1 0.0 reduce-scatter.2.cloned.1.call-start
  37.1 132.0 %all-gather.4.cloned.1.call-done = bf16[1024,3584]{1,0:T(8,128)(2,1)} async-done(((bf16[256,3584]{1,0:T(8,128)(2,1)}), bf16[1024,3584]{1,0:T(8,128)(2,1)}) %all-gather.4.cloned.1.call-update) | async-done | bytes 7340048 | tf_op jit(solution)/shard_map/all_gather | solution.py:12
  169.1 61.3 %fusion.5 = f32[1024,7168]{1,0:T(8,128)} fusion(bf16[1024,3584]{1,0:T(8,128)(2,1)} %all-gather.4.cloned.1.call-done, bf16[3584,7168]{1,0:T(8,128)(2,1)} %param.6), kind=kOutput, calls=%fused_computation.7 | convolution fusion | flops 52613349376 | bytes 88080384 | tf_op jit(solution)/shard_map/dot_general | solution.py:14
  230.5 0.0 reduce-scatter.2.cloned.1.call-update
  230.5 0.0 all-gather.8.cloned.1.call-start
  230.5 0.7 all-gather.8.cloned.1.call-update
  231.2 0.0 all-gather.6.cloned.1.call-start
  231.3 176.4 %reduce-scatter.2.cloned.1.call-done = f32[128,7168]{1,0:T(8,128)} async-done(((f32[1024,7168]{1,0:T(8,128)}), f32[128,7168]{1,0:T(8,128)}) %reduce-scatter.2.cloned.1.call-update) | async-done | bytes 3670032 | tf_op jit(solution)/shard_map/reduce_scatter | solution.py:13
  407.6 3.5 convert_element_type.6
  411.1 0.0 all-gather.6.cloned.1.call-update
  411.2 35.1 %all-gather.8.cloned.1.call-done = bf16[256,8192]{1,0:T(8,128)(2,1)} async-done(((bf16[32,8192]{1,0:T(8,128)(2,1)}), bf16[256,8192]{1,0:T(8,128)(2,1)}) %all-gather.8.cloned.1.call-update) | async-done | bytes 4194320 | tf_op jit(solution)/shard_map/all_gather | solution.py:20
  446.3 6.4 copy.9
  452.6 99.6 %all_to_all.39 = bf16[256,4,2048]{0,2,1:T(8,128)(2,1)} all-to-all(bf16[256,4,2048]{0,2,1:T(8,128)(2,1)} %bitcast.14), channel_id=1, replica_groups=mesh['row'=4,'col'=8] {'row'}, dimensions={1} | all-to-all | bytes 8388608 | tf_op jit(solution)/shard_map/all_to_all | solution.py:21
  552.3 6.2 copy.10
  558.4 9.9 %fusion.6 = f32[1024,1024]{1,0:T(8,128)} fusion(bf16[1024,2048]{1,0:T(8,128)(2,1)} %bitcast.18, bf16[2048,1024]{1,0:T(8,128)(2,1)} %param.7), kind=kOutput, calls=%fused_computation.8 | convolution fusion | flops 4294967296 | bytes 12582912 | tf_op jit(solution)/shard_map/dot_general | solution.py:22
  568.4 145.9 %all-reduce.1 = bf16[1024,1024]{1,0:T(8,128)(2,1)S(1)} all-reduce(f32[1024,1024]{1,0:T(8,128)} %fusion.6), channel_id=1, replica_groups=mesh['row'=4,'col'=8] {'row'}, use_global_device_ids=true, to_apply=%region_1.0 | all-reduce | flops 1048576 | bytes 6291456 | tf_op jit(solution)/shard_map/psum | solution.py:23
  714.3 0.0 all-gather.6.cloned.1.call-done
  714.3 17.4 %fusion.1 = f32[7168,1024]{1,0:T(8,128)} fusion(bf16[1024,7168]{1,0:T(8,128)(2,1)} %all-gather.6.cloned.1.call-done, bf16[1024,1024]{1,0:T(8,128)(2,1)S(1)} %all-reduce.1), kind=kOutput, calls=%fused_computation.2 | convolution fusion | flops 7516192768 | bytes 37748736 | tf_op jit(solution)/shard_map/dot_general | solution.py:28
  731.8 23.1 %add_multiply_fusion = f32[7168,1024]{1,0:T(8,128)} fusion(f32[7168,1024]{1,0:T(8,128)} %fusion.1, bf16[1024,7168]{1,0:T(8,128)(2,1)} %all-gather.6.cloned.1.call-done, bf16[1024,1024]{1,0:T(8,128)(2,1)S(1)} %all-reduce.1), kind=kOutput, calls=%fused_computation | convolution fusion | flops 7545552896 | bytes 67108864 | tf_op jit(solution)/shard_map/dot_general | solution.py:28
Async XLA Ops:
  6.5 162.6 %all-gather.4.cloned.1.call-start = ((), (), s32[]{:S(2)}) async-start(), calls=%async_computation.3 | async-start | bytes 9175040 | tf_op jit(solution)/shard_map/all_gather | solution.py:12
  37.1 370.6 %reduce-scatter.2.cloned.1.call-start = ((), (), s32[]{:S(2)}) async-start(), calls=%async_computation.4 | async-start | bytes 33030144 | tf_op jit(solution)/shard_map/reduce_scatter | solution.py:13
  230.5 215.8 %all-gather.8.cloned.1.call-start = ((), (), s32[]{:S(2)}) async-start(), calls=%async_computation.6 | async-start | bytes 4718592 | tf_op jit(solution)/shard_map/all_gather | solution.py:20
  231.2 483.1 %all-gather.6.cloned.1.call-start = ((), (), s32[]{:S(2)}) async-start(), calls=%async_computation.5 | async-start | bytes 16515072 | tf_op jit(solution)/shard_map/all_gather | solution.py:19
Sparse Core Ops, SparseCore 0:
  37.2 131.8 all-gather.3
  230.6 176.9 reduce-scatter.1
  409.5 36.6 all-gather.7
  448.0 80.9 all-gather.5
where the time goes:
time: 762 us; the launch traced here: 761 us
  waiting for transfers between devices  344 us (45%)
  blocking collectives  274 us (36%)
  matrix products  112 us (15%)
  local copies, waits for them, and re-layouts  14.2 us (2%)
  between operations  13.2 us (2%)
    reduce_scatter x1, waiting for transfers between devices, on_device(): lax.psum_scatter(jnp.dot(whole_acts, act_basis, preferred_element_type=jn...  176 us
    psum x1, blocking collectives, on_device(): rot_grads = lax.psum(partial_grads, 'row').astype(jnp.bfloat16)  146 us
    all_gather x1, waiting for transfers between devices, on_device(): whole_acts = lax.all_gather(local_acts, 'row', axis=0, tiled=True)  132 us
    all_to_all x1, blocking collectives, on_device(): lax.all_to_all(grad_block, 'row', split_axis=1, concat_axis=0, tiled=True)  99.6 us
    dot_general x1, matrix products, on_device(): jnp.dot(whole_acts, act_basis, preferred_element_type=jnp.float32)  61.3 us
    dot_general x2, matrix products, on_device(): lax.dot_general(left, right, (((0,), (0,)), ((), ())), preferred_element_...  40.6 us
    all_gather x1, waiting for transfers between devices, on_device(): grad_block = lax.all_gather(gradients, 'col', axis=0, tiled=True)  35.1 us
    all_to_all x1, blocking collectives, on_device(): lax.all_to_all(activations, 'col', split_axis=1, concat_axis=0, tiled=True)  28.9 us
  transfers between devices with their start and end apart: 4, of which 3 were waited for; matrix products, arithmetic and copies ran while one was open for 3% of the time, Pallas kernels for 0%

commit v1 on v0

v1 whole, which is shorter than its diff:
```python
import functools

import jax
import jax.numpy as jnp
from jax import lax
from jax.experimental import pallas as pl
from jax.experimental.pallas import tpu as pltpu
from jax.sharding import PartitionSpec as P

SEQS = 2
LEN = 512
CHUNKS = 2


def pick(array, index, axis):
    return lax.dynamic_index_in_dim(array, index, axis, keepdims=False)


def sum_shares(partial, cols, stage):
    c = lax.axis_index("col")
    bits = cols.bit_length() - 1
    tokens, width = partial.shape[0], partial.shape[-1]

    def halve(value, held, bit, dtype):
        axis = len(held) - 1 - held.index(bit)
        mine = lax.rem(lax.div(c, 1 << bit), 2)
        sent = pick(value, 1 - mine, axis).astype(dtype)
        kept = pick(value, mine, axis)
        perm = [(i, i ^ (1 << bit)) for i in range(cols)]
        got = lax.ppermute(sent, "col", perm)
        return kept + got.astype(jnp.float32), [b for b in held if b != bit]

    held = list(range(bits))
    if stage == 0:
        value = partial.reshape((2,) * bits + (tokens // cols, width))
        return halve(value, held, 0, jnp.float32)[0]
    value, held = partial, held[1:]
    half = width // 2
    parts = []
    for k, order in enumerate((held, held[::-1])):
        part, left = value[..., k * half : (k + 1) * half], list(held)
        for bit in order:
            part, left = halve(part, left, bit, jnp.bfloat16)
        parts.append(part)
    return jnp.concatenate([p.astype(jnp.bfloat16) for p in parts], axis=-1)


def gather_shares(value, cols):
    c = lax.axis_index("col")
    bits = cols.bit_length() - 1

    def double(part, bit):
        perm = [(i, i ^ (1 << bit)) for i in range(cols)]
        got = lax.ppermute(part, "col", perm)
        upper = lax.rem(lax.div(c, 1 << bit), 2) == 1
        return jnp.stack([jnp.where(upper, got, part), jnp.where(upper, part, got)])

    value = double(value, 0)
    rest = list(range(1, bits))
    half = value.shape[-1] // 2
    parts = []
    for k, order in enumerate((rest, rest[::-1])):
        part = value[..., k * half : (k + 1) * half]
        for bit in order:
            part = double(part, bit)
        axes = [order[::-1].index(bit) for bit in rest[::-1]]
        axes += list(range(len(axes), part.ndim))
        parts.append(part.transpose(axes))
    return jnp.concatenate(parts, axis=-1).reshape((cols,) + value.shape[1:])


def correction_tile(chunks, *refs):
    lefts, right, out = refs[:chunks], refs[chunks], refs[chunks + 1]
    rows, share, width = lefts[0].shape
    per_seq = rows // SEQS
    total = None
    for seq in range(SEQS):
        grad_s = None
        for k in range(chunks):
            left = lefts[k][seq * per_seq : (seq + 1) * per_seq].reshape(per_seq * share, width)
            term = lax.dot_general(
                left, right[k, seq], (((0,), (0,)), ((), ())), preferred_element_type=jnp.float32
            )
            grad_s = term if grad_s is None else grad_s + term
        total = grad_s * grad_s if total is None else total + grad_s * grad_s
    out[...] = total * (1.0 / (SEQS * LEN))


def correct(lefts, right):
    rows, share, height = lefts[0].shape
    tile = next(t for t in (512, 256, 128) if height % t == 0)
    width = right.shape[-1]
    return pl.pallas_call(
        functools.partial(correction_tile, len(lefts)),
        grid=(height // tile,),
        in_specs=[pl.BlockSpec((rows, share, tile), lambda i: (0, 0, i)) for _ in lefts]
        + [pl.BlockSpec(right.shape, lambda i: (0, 0, 0, 0))],
        out_specs=pl.BlockSpec((tile, width), lambda i: (i, 0)),
        out_shape=jax.ShapeDtypeStruct((height, width), jnp.float32),
        compiler_params=pltpu.CompilerParams(vmem_limit_bytes=40 << 20),
    )(*lefts, right)


def on_device(rows, cols, activations, gradients, act_basis, grad_basis):
    r = lax.axis_index("row")

    local_acts = lax.all_to_all(activations, "col", split_axis=1, concat_axis=0, tiled=True)
    tokens = local_acts.shape[0]
    share = tokens // CHUNKS

    tokens_here = gradients.shape[0]
    features = gradients.shape[1] // rows
    cut = lax.all_to_all(
        gradients.reshape(tokens_here, rows, features), "row", split_axis=1, concat_axis=0, tiled=True
    ).reshape(rows, tokens_here, features)
    whole_grads = gather_shares(cut, cols).transpose(1, 0, 2, 3).reshape(rows * tokens, features)

    chunks = [
        lax.all_gather(local_acts[k * share : (k + 1) * share], "row", axis=0, tiled=True)
        for k in range(CHUNKS)
    ]
    chunks[0], whole_grads = lax.optimization_barrier((chunks[0], whole_grads))
    paired = []
    for k in range(CHUNKS):
        if k == CHUNKS - 1:
            partial_grads = jnp.dot(whole_grads, grad_basis, preferred_element_type=jnp.float32)
            partial_grads, chunks[k] = lax.optimization_barrier((partial_grads, chunks[k]))
        partial = jnp.dot(chunks[k], act_basis, preferred_element_type=jnp.float32)
        if k == 0:
            whole_grads, partial = lax.optimization_barrier((whole_grads, partial))
        paired.append(sum_shares(partial, cols, 0))

    partial_grads = partial_grads.reshape(rows, tokens, -1)
    perms = [[(i, (i + shift) % rows) for i in range(rows)] for shift in range(rows)]
    summed = pick(partial_grads, r, 0)
    for shift in range(1, rows):
        sent = pick(partial_grads, lax.rem(r + shift, rows), 0).astype(jnp.bfloat16)
        summed = summed + lax.ppermute(sent, "row", perms[shift]).astype(jnp.float32)
    mine = summed.astype(jnp.bfloat16)

    rotated = []
    for k in range(CHUNKS):
        shares = sum_shares(paired[k], cols, 1)
        if k > 0:
            shares, rotated[k - 1], mine = lax.optimization_barrier((shares, rotated[k - 1], mine))
        whole = lax.all_gather(shares, "col", axis=0, tiled=True)
        rotated.append(whole.reshape(rows, share, -1))

    held = jnp.stack([mine] + [lax.ppermute(mine, "row", perms[shift]) for shift in range(1, rows)])
    rot_grads = jnp.stack([pick(held, lax.rem(r - b + rows, rows), 0) for b in range(rows)])

    per_seq = rows // SEQS
    right = (
        rot_grads.reshape(SEQS, per_seq, CHUNKS, share, -1)
        .transpose(2, 0, 1, 3, 4)
        .reshape(CHUNKS, SEQS, per_seq * share, -1)
    )
    return correct(rotated, right)


def solution(mesh):
    return jax.shard_map(
        functools.partial(on_device, mesh.shape["row"], mesh.shape["col"]),
        mesh=mesh,
        in_specs=(
            P(("row", "col"), None),
            P(("row", "col"), None),
            P("col", "row"),
            P("row", "col"),
        ),
        out_specs=P("row", "col"),
        check_vma=False,
    )
```

time: 762 us -> 442 us (0.58)
  blocking collectives: 274 us -> 59.3 us
  waiting for transfers between devices: 344 us -> 195 us
  matrix products: 112 us -> 77.6 us
  Pallas kernels: 0 us -> 22 us
  other arithmetic: 3.5 us -> 23 us
  local copies, waits for them, and re-layouts: 14.2 us -> 32.7 us
  starting transfers between devices: 0.12 us -> 18 us
    reduce_scatter x1 -> x0, waiting for transfers between devices: 176 us -> none  [on_device(): lax.psum_scatter(jnp.dot(whole_acts, act_basis, preferred_element_type=jn...]
    ppermute x0 -> x21, waiting for transfers between devices: none -> 168 us  [the longest x10 59.8 us: halve(): got = lax.ppermute(sent, 'col', perm)]
    psum x1 -> x0, blocking collectives: 146 us -> none  [on_device(): rot_grads = lax.psum(partial_grads, 'row').astype(jnp.bfloat16)]
    all_gather x3 -> x4, waiting for transfers between devices: 167 us -> 26.5 us  [the longest x2 21.9 us: on_device(): lax.all_gather(local_acts[k * share:(k + 1) * share], 'row', axis=0, tile...]
    all_to_all x1, blocking collectives: 99.6 us -> 30.4 us  [on_device(): lax.all_to_all(gradients.reshape(tokens_here, rows, features), 'row', spl...]
    dot_general x4 -> x3, matrix products: 112 us -> 77.6 us  [the longest x2 67.7 us: on_device(): partial = jnp.dot(chunks[k], act_basis, preferred_element_type=jnp.float32)]
    pallas_call x0 -> x1, Pallas kernels: none -> 22 us  [correct(): pl.pallas_call(functools.partial(correction_tile, len(lefts)), grid=(heig...]
    ppermute x0 -> x21, starting transfers between devices: none -> 17.9 us  [the longest x10 8.88 us: halve(): got = lax.ppermute(sent, 'col', perm)]
  transfers between devices with their start and end apart: 4 -> 25, of which waited for: 3 -> 19; matrix products, arithmetic and copies ran while one was open for 3% -> 26% of each run, Pallas kernels for 0% -> 0%
where the time goes in v1:
time: 442 us; the launch traced here: 441 us
  waiting for transfers between devices  195 us (44%)
  matrix products  77.6 us (18%)
  blocking collectives  59.3 us (13%)
  local copies, waits for them, and re-layouts  32.7 us (7%)
  other arithmetic  23 us (5%)
  Pallas kernels  22 us (5%)
  starting transfers between devices  18 us (4%)
  between operations  13.4 us (3%)
    dot_general x2, matrix products, on_device(): partial = jnp.dot(chunks[k], act_basis, preferred_element_type=jnp.float32)  67.7 us
    ppermute x10, waiting for transfers between devices, halve(): got = lax.ppermute(sent, 'col', perm)  59.8 us
    ppermute x3, waiting for transfers between devices, on_device(): lax.ppermute(mine, 'row', perms[shift])  40.3 us
    ppermute x5, waiting for transfers between devices, double(): got = lax.ppermute(part, 'col', perm)  36.9 us
    ppermute x3, waiting for transfers between devices, on_device(): lax.ppermute(sent, 'row', perms[shift]).astype(jnp.float32)  31.1 us
    all_to_all x1, blocking collectives, on_device(): lax.all_to_all(gradients.reshape(tokens_here, rows, features), 'row', spl...  30.4 us
    all_to_all x1, blocking collectives, on_device(): lax.all_to_all(activations, 'col', split_axis=1, concat_axis=0, tiled=True)  28.9 us
    pallas_call x1, Pallas kernels, correct(): pl.pallas_call(functools.partial(correction_tile, len(lefts)), grid=(heig...  22 us
  transfers between devices with their start and end apart: 25, of which 19 were waited for; matrix products, arithmetic and copies ran while one was open for 26% of the time, Pallas kernels for 0%

profile of v1, /device:TPU:0, one launch (start us, length us, event | category | flops | bytes accessed | tf_op | source)
XLA Modules:
  0.0 440.9 jit_solution(6274283096018162372)
XLA Ops:
  8.2 28.9 %all_to_all.31 = bf16[32,8,3584]{2,0,1:T(8,128)(2,1)S(1)} all-to-all(bf16[32,8,3584]{2,0,1:T(8,128)(2,1)S(1)} %bitcast.136), channel_id=1, replica_groups=mesh['row'=4,'col'=8] {'col'}, dimensions={1} | all-to-all | bytes 3670016 | tf_op jit(solution)/shard_map/all_to_all | solution.py:107
  38.6 30.4 %all_to_all.32 = bf16[32,4,2048]{2,0,1:T(8,128)(2,1)S(1)} all-to-all(bf16[32,4,2048]{2,0,1:T(8,128)(2,1)S(1)} %bitcast.142), channel_id=1, replica_groups=mesh['row'=4,'col'=8] {'row'}, dimensions={1} | all-to-all | bytes 1048576 | tf_op jit(solution)/shard_map/all_to_all | solution.py:113
  72.6 12.5 %collective-permute-done.3 = bf16[2,4,32,1024]{3,2,1,0:T(8,128)(2,1)S(1)} collective-permute-done((bf16[2,4,32,1024]{3,2,1,0:T(8,128)(2,1)S(1)}, bf16[2,4,32,1024]{3,2,1,0:T(8,128)(2,1)S(1)}, u32[]{:S(2)}, u32[]{:S(2)}) %collective-permute-start.3) | collective-permute-done | bytes 524320 | tf_op jit(solution)/shard_map/ppermute | solution.py:54
  89.1 22.0 %collective-permute-done.4 = bf16[2,2,4,32,1024]{4,3,2,1,0:T(8,128)(2,1)} collective-permute-done((bf16[2,2,4,32,1024]{4,3,2,1,0:T(8,128)(2,1)}, bf16[2,2,4,32,1024]{4,3,2,1,0:T(8,128)(2,1)}, u32[]{:S(2)}, u32[]{:S(2)}) %collective-permute-start.4) | collective-permute-done | bytes 1048608 | tf_op jit(solution)/shard_map/ppermute | solution.py:54
  116.8 32.9 %fusion.22 = f32[512,7168]{1,0:T(8,128)S(1)} fusion(bf16[512,3584]{1,0:T(8,128)(2,1)} %all-gather.5.cloned.1.call-done, bf16[3584,7168]{1,0:T(8,128)(2,1)} %param.6), kind=kOutput, calls=%fused_computation.73 | convolution fusion | flops 26306674688 | bytes 69730304 | tf_op jit(solution)/shard_map/dot_general | solution.py:128
  149.7 4.1 dynamic-slice_bitcast_fusion
  157.4 9.9 %fusion.23 = f32[1024,1024]{1,0:T(8,128)} fusion(bf16[1024,2048]{1,0:T(8,128)(2,1)} %bitcast.138, bf16[2048,1024]{1,0:T(8,128)(2,1)} %param.7), kind=kOutput, calls=%fused_computation.74 | convolution fusion | flops 4294967296 | bytes 12582912 | tf_op jit(solution)/shard_map/dot_general | solution.py:126
  167.4 21.1 %all-gather.7.cloned.1.call-done = bf16[512,3584]{1,0:T(8,128)(2,1)} async-done(((bf16[128,3584]{1,0:T(8,128)(2,1)}), bf16[512,3584]{1,0:T(8,128)(2,1)}) %all-gather.7.cloned.1.call-update) | async-done | bytes 3670032 | tf_op jit(solution)/shard_map/all_gather | solution.py:119
  188.5 34.8 %fusion.24 = f32[512,7168]{1,0:T(8,128)} fusion(bf16[512,3584]{1,0:T(8,128)(2,1)} %all-gather.7.cloned.1.call-done, bf16[3584,7168]{1,0:T(8,128)(2,1)} %param.6), kind=kOutput, calls=%fused_computation.75 | convolution fusion | flops 26306674688 | bytes 69730304 | tf_op jit(solution)/shard_map/dot_general | solution.py:128
  223.3 6.3 %bitcast_add_fusion = f32[2,2,64,7168]{3,2,1,0:T(8,128)S(1)} fusion(f32[2,2,64,7168]{3,2,1,0:T(8,128)} %collective-permute-done.10, f32[2,2,2,64,7168]{4,3,2,1,0:T(8,128)} %bitcast.133, s32[]{:T(128)S(6)} %select_n.127), kind=kLoop, calls=%fused_computation | loop fusion | flops 1835008 | bytes 22020100 | tf_op jit(solution)/shard_map/add | solution.py:31
  231.9 6.9 %dynamic-slice_bitcast_fusion.1 = f32[2,2,64,7168]{3,2,1,0:T(8,128)} fusion(f32[2,2,2,64,7168]{4,3,2,1,0:T(8,128)} %bitcast.130, s32[]{:T(128)S(6)} %select_n.128), kind=kLoop, calls=%fused_computation.3 | loop fusion | bytes 14680068 | tf_op jit(solution)/shard_map/jit(dynamic_index_in_dim)/squeeze | solution.py:16
  240.5 12.0 %collective-permute-done.13 = bf16[2,64,3584]{2,1,0:T(8,128)(2,1)S(1)} collective-permute-done((bf16[2,64,3584]{2,1,0:T(8,128)(2,1)S(1)}, bf16[2,64,3584]{2,1,0:T(8,128)(2,1)S(1)}, u32[]{:S(2)}, u32[]{:S(2)}) %collective-permute-start.13) | collective-permute-done | bytes 917536 | tf_op jit(solution)/shard_map/ppermute | solution.py:30
  254.3 7.9 %collective-permute-done.11 = bf16[2,64,3584]{2,1,0:T(8,128)(2,1)S(1)} collective-permute-done((bf16[2,64,3584]{2,1,0:T(8,128)(2,1)S(1)}, bf16[2,64,3584]{2,1,0:T(8,128)(2,1)S(1)}, u32[]{:S(2)}, u32[]{:S(2)}) %collective-permute-start.11) | collective-permute-done | bytes 917536 | tf_op jit(solution)/shard_map/ppermute | solution.py:30
  263.0 8.6 %collective-permute-done.14 = bf16[64,3584]{1,0:T(8,128)(2,1)S(1)} collective-permute-done((bf16[64,3584]{1,0:T(8,128)(2,1)S(1)}, bf16[64,3584]{1,0:T(8,128)(2,1)S(1)}, u32[]{:S(2)}, u32[]{:S(2)}) %collective-permute-start.14) | collective-permute-done | bytes 458784 | tf_op jit(solution)/shard_map/ppermute | solution.py:30
  277.6 3.8 collective-permute-start.17
  281.4 6.6 %bitcast_add_fusion.1 = f32[2,2,64,7168]{3,2,1,0:T(8,128)S(1)} fusion(f32[2,2,64,7168]{3,2,1,0:T(8,128)} %collective-permute-done.5, f32[2,2,2,64,7168]{4,3,2,1,0:T(8,128)} %bitcast.131, s32[]{:T(128)S(6)} %select_n.127), kind=kLoop, calls=%fused_computation.1 | loop fusion | flops 1835008 | bytes 22020100 | tf_op jit(solution)/shard_map/add | solution.py:31
  294.4 7.0 %collective-permute-done.17 = bf16[256,1024]{1,0:T(8,128)(2,1)} collective-permute-done((bf16[256,1024]{1,0:T(8,128)(2,1)S(1)}, bf16[256,1024]{1,0:T(8,128)(2,1)}, u32[]{:S(2)}, u32[]{:S(2)}) %collective-permute-start.17) | collective-permute-done | bytes 524320 | tf_op jit(solution)/shard_map/ppermute | solution.py:138
  301.4 23.0 %collective-permute-done.16 = bf16[256,1024]{1,0:T(8,128)(2,1)} collective-permute-done((bf16[256,1024]{1,0:T(8,128)(2,1)S(1)}, bf16[256,1024]{1,0:T(8,128)(2,1)}, u32[]{:S(2)}, u32[]{:S(2)}) %collective-permute-start.16) | collective-permute-done | bytes 524320 | tf_op jit(solution)/shard_map/ppermute | solution.py:138
  330.6 20.9 %collective-permute-done.6 = bf16[2,64,3584]{2,1,0:T(8,128)(2,1)S(1)} collective-permute-done((bf16[2,64,3584]{2,1,0:T(8,128)(2,1)S(1)}, bf16[2,64,3584]{2,1,0:T(8,128)(2,1)S(1)}, u32[]{:S(2)}, u32[]{:S(2)}) %collective-permute-start.6) | collective-permute-done | bytes 917536 | tf_op jit(solution)/shard_map/ppermute | solution.py:30
  352.4 6.8 %collective-permute-done.9 = bf16[64,3584]{1,0:T(8,128)(2,1)S(1)} collective-permute-done((bf16[64,3584]{1,0:T(8,128)(2,1)S(1)}, bf16[64,3584]{1,0:T(8,128)(2,1)S(1)}, u32[]{:S(2)}, u32[]{:S(2)}) %collective-permute-start.9) | collective-permute-done | bytes 458784 | tf_op jit(solution)/shard_map/ppermute | solution.py:30
  363.5 11.5 %collective-permute-done.20 = bf16[256,1024]{1,0:T(8,128)(2,1)S(1)} collective-permute-done((bf16[256,1024]{1,0:T(8,128)(2,1)S(1)}, bf16[256,1024]{1,0:T(8,128)(2,1)S(1)}, u32[]{:S(2)}, u32[]{:S(2)}) %collective-permute-start.20) | collective-permute-done | bytes 524320 | tf_op jit(solution)/shard_map/ppermute | solution.py:149
  375.0 28.8 %collective-permute-done.19 = bf16[256,1024]{1,0:T(8,128)(2,1)S(1)} collective-permute-done((bf16[256,1024]{1,0:T(8,128)(2,1)S(1)}, bf16[256,1024]{1,0:T(8,128)(2,1)S(1)}, u32[]{:S(2)}, u32[]{:S(2)}) %collective-permute-start.19) | collective-permute-done | bytes 524320 | tf_op jit(solution)/shard_map/ppermute | solution.py:149
  404.7 4.6 %all-gather.11.cloned.1.call-done = bf16[512,7168]{1,0:T(8,128)(2,1)} async-done(((bf16[64,7168]{1,0:T(8,128)(2,1)}), bf16[512,7168]{1,0:T(8,128)(2,1)}) %all-gather.11.cloned.1.call-update) | async-done | bytes 7340048 | tf_op jit(solution)/shard_map/all_gather | solution.py:146
  412.4 22.0 %shard_map.46 = f32[7168,1024]{1,0:T(8,128)} custom-call(bf16[4,128,7168]{2,1,0:T(8,128)(2,1)S(1)} %bitcast.128, bf16[4,128,7168]{2,1,0:T(8,128)(2,1)} %bitcast.137, bf16[2,2,256,1024]{3,2,1,0:T(8,128)(2,1)S(1)} %bitcast.127), custom_call_target="tpu_custom_call" | custom-call | tf_op jit(solution)/shard_map/pallas_call | solution.py:93
  (92 shorter events, 54.1 us)
Async XLA Ops:
  6.5 110.3 %all-gather.5.cloned.1.call-start = ((), (), s32[]{:S(2)}) async-start(), calls=%async_computation.2 | async-start | bytes 4587520 | tf_op jit(solution)/shard_map/all_gather | solution.py:119
  38.5 150.0 %all-gather.7.cloned.1.call-start = ((), (), s32[]{:S(2)}) async-start(), calls=%async_computation.3 | async-start | bytes 4587520 | tf_op jit(solution)/shard_map/all_gather | solution.py:119
  71.1 14.0 %collective-permute-start.3 = (bf16[2,4,32,1024]{3,2,1,0:T(8,128)(2,1)S(1)}, bf16[2,4,32,1024]{3,2,1,0:T(8,128)(2,1)S(1)}, u32[]{:S(2)}, u32[]{:S(2)}) collective-permute-start(bf16[2,4,32,1024]{3,2,1,0:T(8,128)(2,1)S(1)} %get-tuple-element.43), channel_id=1, source_target_pairs={{0,4},{1,5},{2,6},{3,7},{4,0},{5,1},{6,2},{7,3},{8,12},{9,13},{10,... | collective-permute-start | bytes 1572872 | tf_op jit(solution)/shard_map/ppermute | solution.py:54
  71.7 15.9 %collective-permute-start.1 = (bf16[2,4,32,1024]{3,2,1,0:T(8,128)(2,1)S(1)}, bf16[2,4,32,1024]{3,2,1,0:T(8,128)(2,1)S(1)}, u32[]{:S(2)}, u32[]{:S(2)}) collective-permute-start(bf16[2,4,32,1024]{3,2,1,0:T(8,128)(2,1)S(1)} %get-tuple-element.42), channel_id=1, source_target_pairs={{0,2},{1,3},{2,0},{3,1},{4,6},{5,7},{6,4},{7,5},{8,10},{9,11},{10,... | collective-permute-start | bytes 1572872 | tf_op jit(solution)/shard_map/ppermute | solution.py:54
  86.3 24.8 %collective-permute-start.4 = (bf16[2,2,4,32,1024]{4,3,2,1,0:T(8,128)(2,1)}, bf16[2,2,4,32,1024]{4,3,2,1,0:T(8,128)(2,1)}, u32[]{:S(2)}, u32[]{:S(2)}) collective-permute-start(bf16[2,2,4,32,1024]{4,3,2,1,0:T(8,128)(2,1)} %pad_maximum_fusion.4), channel_id=1, source_target_pairs={{0,2},{1,3},{2,0},{3,1},{4,6},{5,7},{6,4},{7,5},{8,10},{9,11},{10,... | collective-permute-start | bytes 3145736 | tf_op jit(solution)/shard_map/ppermute | solution.py:54
  88.8 24.4 %collective-permute-start.2 = (bf16[2,2,4,32,1024]{4,3,2,1,0:T(8,128)(2,1)}, bf16[2,2,4,32,1024]{4,3,2,1,0:T(8,128)(2,1)S(1)}, u32[]{:S(2)}, u32[]{:S(2)}) collective-permute-start(bf16[2,2,4,32,1024]{4,3,2,1,0:T(8,128)(2,1)} %pad_maximum_fusion.3), channel_id=1, source_target_pairs={{0,4},{1,5},{2,6},{3,7},{4,0},{5,1},{6,2},{7,3},{8,12},{9,13},{10,... | collective-permute-start | bytes 3145736 | tf_op jit(solution)/shard_map/ppermute | solution.py:54
  89.1 272.3 %all-gather.9.cloned.1.call-start = ((), (), s32[]{:S(2)}) async-start(), calls=%async_computation.4 | async-start | bytes 8257536 | tf_op jit(solution)/shard_map/all_gather | solution.py:146
  157.4 65.9 %collective-permute-start.10 = (f32[2,2,64,7168]{3,2,1,0:T(8,128)}, f32[2,2,64,7168]{3,2,1,0:T(8,128)}, u32[]{:S(2)}, u32[]{:S(2)}) collective-permute-start(f32[2,2,64,7168]{3,2,1,0:T(8,128)} %dynamic-slice_bitcast_fusion), channel_id=1, source_target_pairs={{0,1},{1,0},{2,3},{3,2},{4,5},{5,4},{6,7},{7,6},{8,9},{9,8},{10,11... | collective-permute-start | bytes 22020104 | tf_op jit(solution)/shard_map/ppermute | solution.py:30
  230.3 22.2 %collective-permute-start.13 = (bf16[2,64,3584]{2,1,0:T(8,128)(2,1)S(1)}, bf16[2,64,3584]{2,1,0:T(8,128)(2,1)S(1)}, u32[]{:S(2)}, u32[]{:S(2)}) collective-permute-start(bf16[2,64,3584]{2,1,0:T(8,128)(2,1)S(1)} %fusion.6), channel_id=1, source_target_pairs={{0,4},{1,5},{2,6},{3,7},{4,0},{5,1},{6,2},{7,3},{8,12},{9,13},{10,... | collective-permute-start | bytes 2752520 | tf_op jit(solution)/shard_map/ppermute | solution.py:30
  238.8 42.6 %collective-permute-start.5 = (f32[2,2,64,7168]{3,2,1,0:T(8,128)}, f32[2,2,64,7168]{3,2,1,0:T(8,128)}, u32[]{:S(2)}, u32[]{:S(2)}) collective-permute-start(f32[2,2,64,7168]{3,2,1,0:T(8,128)} %dynamic-slice_bitcast_fusion.1), channel_id=1, source_target_pairs={{0,1},{1,0},{2,3},{3,2},{4,5},{5,4},{6,7},{7,6},{8,9},{9,8},{10,11... | collective-permute-start | bytes 22020104 | tf_op jit(solution)/shard_map/ppermute | solution.py:30
  238.9 23.2 %collective-permute-start.11 = (bf16[2,64,3584]{2,1,0:T(8,128)(2,1)S(1)}, bf16[2,64,3584]{2,1,0:T(8,128)(2,1)S(1)}, u32[]{:S(2)}, u32[]{:S(2)}) collective-permute-start(bf16[2,64,3584]{2,1,0:T(8,128)(2,1)S(1)} %fusion.5), channel_id=1, source_target_pairs={{0,2},{1,3},{2,0},{3,1},{4,6},{5,7},{6,4},{7,5},{8,10},{9,11},{10,... | collective-permute-start | bytes 2752520 | tf_op jit(solution)/shard_map/ppermute | solution.py:30
  252.7 18.9 %collective-permute-start.14 = (bf16[64,3584]{1,0:T(8,128)(2,1)S(1)}, bf16[64,3584]{1,0:T(8,128)(2,1)S(1)}, u32[]{:S(2)}, u32[]{:S(2)}) collective-permute-start(bf16[64,3584]{1,0:T(8,128)(2,1)S(1)} %fusion.18), channel_id=1, source_target_pairs={{0,2},{1,3},{2,0},{3,1},{4,6},{5,7},{6,4},{7,5},{8,10},{9,11},{10,... | collective-permute-start | bytes 1376264 | tf_op jit(solution)/shard_map/ppermute | solution.py:30
  262.4 11.8 %collective-permute-start.12 = (bf16[64,3584]{1,0:T(8,128)(2,1)S(1)}, bf16[64,3584]{1,0:T(8,128)(2,1)S(1)}, u32[]{:S(2)}, u32[]{:S(2)}) collective-permute-start(bf16[64,3584]{1,0:T(8,128)(2,1)S(1)} %fusion.17), channel_id=1, source_target_pairs={{0,4},{1,5},{2,6},{3,7},{4,0},{5,1},{6,2},{7,3},{8,12},{9,13},{10,... | collective-permute-start | bytes 1376264 | tf_op jit(solution)/shard_map/ppermute | solution.py:30
  275.4 134.0 %all-gather.11.cloned.1.call-start = ((), (), s32[]{:S(2)}) async-start(), calls=%async_computation.5 | async-start | bytes 8257536 | tf_op jit(solution)/shard_map/all_gather | solution.py:146
  277.5 16.8 %collective-permute-start.15 = (bf16[256,1024]{1,0:T(8,128)(2,1)S(1)}, bf16[256,1024]{1,0:T(8,128)(2,1)}, u32[]{:S(2)}, u32[]{:S(2)}) collective-permute-start(bf16[256,1024]{1,0:T(8,128)(2,1)S(1)} %get-tuple-element.27), channel_id=1, source_target_pairs={{0,8},{8,16},{16,24},{24,0},{1,9},{9,17},{17,25},{25,1},{2,10},{10... | collective-permute-start | bytes 1572872 | tf_op jit(solution)/shard_map/ppermute | solution.py:138
  277.6 23.8 %collective-permute-start.17 = (bf16[256,1024]{1,0:T(8,128)(2,1)S(1)}, bf16[256,1024]{1,0:T(8,128)(2,1)}, u32[]{:S(2)}, u32[]{:S(2)}) collective-permute-start(bf16[256,1024]{1,0:T(8,128)(2,1)S(1)} %get-tuple-element.28), channel_id=1, source_target_pairs={{0,24},{8,0},{16,8},{24,16},{1,25},{9,1},{17,9},{25,17},{2,26},{10... | collective-permute-start | bytes 1572872 | tf_op jit(solution)/shard_map/ppermute | solution.py:138
  281.4 42.9 %collective-permute-start.16 = (bf16[256,1024]{1,0:T(8,128)(2,1)S(1)}, bf16[256,1024]{1,0:T(8,128)(2,1)}, u32[]{:S(2)}, u32[]{:S(2)}) collective-permute-start(bf16[256,1024]{1,0:T(8,128)(2,1)S(1)} %get-tuple-element.29), channel_id=1, source_target_pairs={{0,16},{8,24},{16,0},{24,8},{1,17},{9,25},{17,1},{25,9},{2,18},{10... | collective-permute-start | bytes 1572872 | tf_op jit(solution)/shard_map/ppermute | solution.py:138
  292.4 37.3 %collective-permute-start.8 = (bf16[2,64,3584]{2,1,0:T(8,128)(2,1)S(1)}, bf16[2,64,3584]{2,1,0:T(8,128)(2,1)S(1)}, u32[]{:S(2)}, u32[]{:S(2)}) collective-permute-start(bf16[2,64,3584]{2,1,0:T(8,128)(2,1)S(1)} %fusion.4), channel_id=1, source_target_pairs={{0,4},{1,5},{2,6},{3,7},{4,0},{5,1},{6,2},{7,3},{8,12},{9,13},{10,... | collective-permute-start | bytes 2752520 | tf_op jit(solution)/shard_map/ppermute | solution.py:30
  328.1 23.4 %collective-permute-start.6 = (bf16[2,64,3584]{2,1,0:T(8,128)(2,1)S(1)}, bf16[2,64,3584]{2,1,0:T(8,128)(2,1)S(1)}, u32[]{:S(2)}, u32[]{:S(2)}) collective-permute-start(bf16[2,64,3584]{2,1,0:T(8,128)(2,1)S(1)} %fusion.3), channel_id=1, source_target_pairs={{0,2},{1,3},{2,0},{3,1},{4,6},{5,7},{6,4},{7,5},{8,10},{9,11},{10,... | collective-permute-start | bytes 2752520 | tf_op jit(solution)/shard_map/ppermute | solution.py:30
  330.0 29.2 %collective-permute-start.9 = (bf16[64,3584]{1,0:T(8,128)(2,1)S(1)}, bf16[64,3584]{1,0:T(8,128)(2,1)S(1)}, u32[]{:S(2)}, u32[]{:S(2)}) collective-permute-start(bf16[64,3584]{1,0:T(8,128)(2,1)S(1)} %fusion.16), channel_id=1, source_target_pairs={{0,2},{1,3},{2,0},{3,1},{4,6},{5,7},{6,4},{7,5},{8,10},{9,11},{10,... | collective-permute-start | bytes 1376264 | tf_op jit(solution)/shard_map/ppermute | solution.py:30
  351.7 8.5 %collective-permute-start.7 = (bf16[64,3584]{1,0:T(8,128)(2,1)S(1)}, bf16[64,3584]{1,0:T(8,128)(2,1)S(1)}, u32[]{:S(2)}, u32[]{:S(2)}) collective-permute-start(bf16[64,3584]{1,0:T(8,128)(2,1)S(1)} %fusion.15), channel_id=1, source_target_pairs={{0,4},{1,5},{2,6},{3,7},{4,0},{5,1},{6,2},{7,3},{8,12},{9,13},{10,... | collective-permute-start | bytes 1376264 | tf_op jit(solution)/shard_map/ppermute | solution.py:30
  361.4 13.6 %collective-permute-start.20 = (bf16[256,1024]{1,0:T(8,128)(2,1)S(1)}, bf16[256,1024]{1,0:T(8,128)(2,1)S(1)}, u32[]{:S(2)}, u32[]{:S(2)}) collective-permute-start(bf16[256,1024]{1,0:T(8,128)(2,1)S(1)} %fusion.2), channel_id=1, source_target_pairs={{0,24},{8,0},{16,8},{24,16},{1,25},{9,1},{17,9},{25,17},{2,26},{10... | collective-permute-start | bytes 1572872 | tf_op jit(solution)/shard_map/ppermute | solution.py:149
  362.6 41.2 %collective-permute-start.19 = (bf16[256,1024]{1,0:T(8,128)(2,1)S(1)}, bf16[256,1024]{1,0:T(8,128)(2,1)S(1)}, u32[]{:S(2)}, u32[]{:S(2)}) collective-permute-start(bf16[256,1024]{1,0:T(8,128)(2,1)S(1)} %fusion.2), channel_id=1, source_target_pairs={{0,16},{8,24},{16,0},{24,8},{1,17},{9,25},{17,1},{25,9},{2,18},{10... | collective-permute-start | bytes 1572872 | tf_op jit(solution)/shard_map/ppermute | solution.py:149
  362.6 41.2 %collective-permute-start.18 = (bf16[256,1024]{1,0:T(8,128)(2,1)S(1)}, bf16[256,1024]{1,0:T(8,128)(2,1)S(1)}, u32[]{:S(2)}, u32[]{:S(2)}) collective-permute-start(bf16[256,1024]{1,0:T(8,128)(2,1)S(1)} %fusion.2), channel_id=1, source_target_pairs={{0,8},{8,16},{16,24},{24,0},{1,9},{9,17},{17,25},{25,1},{2,10},{10... | collective-permute-start | bytes 1572872 | tf_op jit(solution)/shard_map/ppermute | solution.py:149
  (7 other events, 106.5 us)
Sparse Core Ops, SparseCore 0:
  38.6 78.1 all-gather.4
  118.4 70.0 all-gather.6
  275.5 59.6 all-gather.8
  361.5 47.7 all-gather.10
